TPU v7x, 32 devices: a whole 2x2x4 slice. The times are simulated.
32 devices in a mesh: row: 16 (over z, x, core), col: 2 (over y).
Axes of the slice: x: 2, y: 2, z: 4, core: 2. Of those that a mesh axis runs over, the one named last changes fastest.
Arguments:
- a_blocks: bfloat16 [16, 2, 16, 128, 128], P('row', 'col'), may hold values from -6 to 6
- a_rows: int32 [16, 2, 16], P('row', 'col'), may hold values from 0 to 3
- b_blocks: bfloat16 [16, 2, 32, 128, 128], P('row', 'col'), may hold values from -0.25 to 0.25
- b_cols: int32 [16, 2, 32], P('row', 'col'), may hold values from 0 to 7
- pair_list: int32 [16, 2, 4, 2, 256], P('row', 'col'), may hold values from 0 to 31, as said below
- pair_count: int32 [16, 2, 4], P('row', 'col'), may hold values from 1 to 256, as said below
- row_order: int32 [16, 4], P('row'), may hold values from 0 to 3, each once within a row
Outputs:
- product_matrix: bfloat16 [8192, 2048], P('row', 'col')
Inputs may be any that keep to these rules, and one draw needn't show every extreme that they name: pair_list[..., 0, :] names a left slot below 16 and pair_list[..., 1, :] a right slot below 32; no list of one device and stop names the same pair twice. `pair_count`: in every stop some device's list is full.
All inputs are finite; a program needn't handle non-finite values.
Results may differ from a plain program's by a relative error of at most 0.001.
Values may be sent and summed in bfloat16 or wider, within the bound.
No kernel may reach another device: no remote copies, remote signals or barrier semaphores. Data moves between devices by JAX's collectives and lax.ppermute only.
A program may use at most 64 MiB of HBM per device.

v0:
```python
import functools

import jax
import jax.numpy as jnp
from jax import lax
from jax.experimental import pallas as pl
from jax.experimental.pallas import tpu as pltpu
from jax.sharding import PartitionSpec as P

CCOLS = 8
PARTS = 2
FIRST_PART = 15, 32
UNROLL = 32
HEAD = 32
HEAD_STEP = 16
VMEM_BYTES = 40 << 20
VMEM = pl.BlockSpec(memory_space=pltpu.VMEM)


def round_up(value, step):
    return value + -value % step


class Sizes:
    def __init__(self, n_stops, n_pairs, n_left, n_right, n_rows, n_col, edge):
        self.n_stops, self.n_pairs, self.n_rows, self.n_col = n_stops, n_pairs, n_rows, n_col
        self.n_left, self.n_right, self.edge = n_left, n_right, edge
        self.parts = PARTS
        first = n_right * FIRST_PART[0] // FIRST_PART[1]
        self.cuts = (0, first, n_right)
        self.per_part = max(first, n_right - first)
        self.zero_slot = n_col * n_left
        self.row_bits = (n_rows - 1).bit_length()
        self.key_bits = self.row_bits + (self.per_part - 1).bit_length()
        self.left_bits = self.zero_slot.bit_length()
        most = (n_pairs + self.per_part * n_rows) // 2
        self.width = round_up(round_up(most, UNROLL) + 1, 128)


def kernel_call(
    kernel,
    out_shape,
    operands,
    scalars=(),
    scratch=(),
    specs=None,
    flops=128,
):
    return pl.pallas_call(
        kernel,
        out_shape=out_shape,
        grid_spec=pltpu.PrefetchScalarGridSpec(
            num_scalar_prefetch=len(scalars),
            in_specs=specs or [VMEM] * len(operands),
            out_specs=jax.tree.map(lambda _: VMEM, out_shape),
            scratch_shapes=list(scratch),
        ),
        compiler_params=pltpu.CompilerParams(vmem_limit_bytes=VMEM_BYTES),
        cost_estimate=pl.CostEstimate(flops=flops, bytes_accessed=128, transcendentals=0),
    )(*scalars, *operands)


def pack_kernel(cuts, blocks_ref, ids_ref, *refs):
    part_refs, head_ref, sems = refs[:-2], refs[-2], refs[-1]
    edge = blocks_ref.shape[1]
    copies = []
    for part, ref in enumerate(part_refs):
        low, count = cuts[part] * edge, (cuts[part + 1] - cuts[part]) * edge
        source, target = blocks_ref.at[pl.ds(low, count)], ref.at[pl.ds(HEAD, count)]
        copies.append(pltpu.make_async_copy(source, target, sems.at[part]))
    for copy in copies:
        copy.start()
    head_ref[...] = jnp.zeros_like(head_ref)
    head_ref[0:1, : ids_ref.shape[1]] = ids_ref[...].astype(jnp.float32)
    for ref in part_refs:
        for row in range(0, HEAD, HEAD_STEP):
            ref[row : row + HEAD_STEP, :] = head_ref[...].astype(ref.dtype)
    for copy in copies:
        copy.wait()


def pack(sizes, blocks, ids):
    edge = sizes.edge
    counts = [high - low for low, high in zip(sizes.cuts, sizes.cuts[1:])]
    shapes = [(HEAD + count * edge, edge) for count in counts]
    return kernel_call(
        functools.partial(pack_kernel, sizes.cuts),
        [jax.ShapeDtypeStruct(shape, blocks.dtype) for shape in shapes],
        [blocks.reshape(-1, edge), ids.reshape(1, -1)],
        scratch=[pltpu.VMEM((HEAD_STEP, edge), jnp.float32), pltpu.SemaphoreType.DMA((PARTS,))],
        specs=[pl.BlockSpec(memory_space=pl.ANY), VMEM],
    )


def ids_of(ref):
    return ref[:HEAD_STEP, :].astype(jnp.float32)[0:1, :]


def prepare_kernel(sizes, count_ref, order_ref, pairs_ref, *refs):
    words_ref = refs[-1]
    id_sets = [ref[...] for ref in refs[:-1]]
    n_col, n_rows, parts = sizes.n_col, sizes.n_rows, sizes.parts
    n_pairs, width = sizes.n_pairs, sizes.width

    def total(mask, value, axis):
        return jnp.sum(jnp.where(mask, value, 0.0), axis=axis, keepdims=True)

    here = lax.axis_index("row")
    lane = lax.broadcasted_iota(jnp.int32, (n_pairs, 128), 1)
    slot = lane[:, : sizes.n_left]
    down = lax.broadcasted_iota(jnp.int32, (n_pairs, 1), 0)
    across = lax.broadcasted_iota(jnp.int32, (1, n_pairs), 1)
    places = lax.broadcasted_iota(jnp.int32, (1, width), 1).astype(jnp.float32)
    dead = float(sizes.n_right * n_rows)
    lefts, keys = [], []
    key_matrix = jnp.zeros((n_pairs, 128), jnp.float32)
    for stop in range(sizes.n_stops):
        ahead = lax.rem(here + stop, n_col)
        ids = id_sets[0]
        for j in range(1, n_col):
            ids = jnp.where(ahead == j, id_sets[j], ids)
        left_row = jnp.zeros(ids.shape, jnp.float32)
        for i in range(n_rows):
            left_row = jnp.where(ids == i, order_ref[:, i : i + 1].astype(jnp.float32), left_row)
        left = pairs_ref[:, 2 * stop : 2 * stop + 1]
        right = pairs_ref[:, 2 * stop + 1 : 2 * stop + 2]
        key = right.astype(jnp.float32) * n_rows + total(slot == left, left_row, 1)
        key = jnp.where(down < count_ref[:, stop : stop + 1], key, dead)
        lefts.append((left + ahead * sizes.n_left - sizes.zero_slot).astype(jnp.float32))
        keys.append(key)
        key_matrix = jnp.where(lane == stop, key, key_matrix)
    key_rows = key_matrix.T
    cut = float(sizes.cuts[1] * n_rows)

    def part_of(key):
        return jnp.where(key >= cut, 1.0, 0.0)

    scale = [float(1 << sizes.key_bits), float(1 << (sizes.key_bits + sizes.left_bits))]
    empty = sizes.zero_slot * (scale[0] + scale[1])
    for stop in range(sizes.n_stops):
        left, key, other = lefts[stop], keys[stop], key_rows[stop : stop + 1, :]
        same = key == other
        rank = total(same & (across < down), 1.0, 1)
        other_rank = total(same & (down < across), 1.0, 0)
        other_opens = other_rank == 2.0 * jnp.floor(other_rank * 0.5)
        own_part, other_part = part_of(key), part_of(other)
        group = jnp.floor(rank * 0.5)
        opens = rank == 2.0 * group
        group += total((other < key) & (own_part == other_part) & other_opens, 1.0, 1)
        word = jnp.where(opens, left * scale[0] + key - own_part * cut, left * scale[1])
        for part in range(parts):
            counted = (own_part == float(part)) & (key < dead)
            words = empty + total(counted & (group == places), word, 0)
            words = jnp.where(places == width - 1.0, total(counted & opens, 1.0, 0), words)
            line = parts * stop + part
            words_ref[line : line + 1, :] = words.astype(jnp.int32)


def products_kernel(sizes, n_rights, layout, opens, closes, words_ref, *refs):
    n_sources = sizes.n_col if opens else 1
    sources, refs = refs[:n_sources], refs[n_sources:]
    right_refs, refs = refs[:n_rights], refs[n_rights:]
    start_ref = None
    if not opens:
        start_ref, refs = refs[0], refs[1:]
    out_ref, refs = refs[0], refs[1:]
    left_ref = sources[0]
    edge = sizes.edge
    if opens:
        left_ref, refs = refs[0], refs[1:]
        rows = sizes.n_left * edge
        for j, source in enumerate(sources):
            left_ref[j * rows : (j + 1) * rows, :] = source[...]
        left_ref[len(sources) * rows :, :] = jnp.zeros((edge, edge), left_ref.dtype)
    ids_ref, col_ref, copy_sem = refs[:3]
    total_ref = refs[3] if closes else out_ref
    for which, ref in enumerate(right_refs):
        ids_ref[which : which + 1, :] = ids_of(ref).astype(jnp.int32)
    copy = pltpu.make_async_copy(ids_ref, col_ref, copy_sem)
    copy.start()
    total_ref[...] = jnp.zeros_like(total_ref) if opens else start_ref[...]
    copy.wait()

    core, col = lax.rem(lax.axis_index("row"), 2), lax.axis_index("col")

    def block(ref, slot, head):
        return ref[pl.ds(pl.multiple_of(slot * edge + head, HEAD_STEP), edge), :]

    for array, head, part, ahead in layout:
        stop = jnp.where(
            core == 0,
            -1 if ahead[0] is None else ahead[0] - col,
            -1 if ahead[1] is None else ahead[1] - col,
        )
        used = (stop >= 0) & (stop < sizes.n_stops)
        line = jnp.clip(stop, 0, sizes.n_stops - 1) * sizes.parts + part
        count = jnp.where(used, words_ref[line, sizes.width - 1], 0)

        def groups(first, size, array=array, head=head, part=part, line=line):
            for member in range(size):
                word = words_ref[line, first + member]
                row = word & ((1 << sizes.row_bits) - 1)
                slot = (word & ((1 << sizes.key_bits) - 1)) >> sizes.row_bits
                word = word >> sizes.key_bits
                lefts = word & ((1 << sizes.left_bits) - 1), word >> sizes.left_bits
                target = row * CCOLS + col_ref[array, slot + sizes.cuts[part]]
                right = block(right_refs[array], slot, head)
                total_ref[target] += jnp.dot(
                    jnp.concatenate([block(left_ref, left, 0) for left in lefts], axis=1),
                    jnp.concatenate([right, right], axis=0),
                    preferred_element_type=jnp.float32,
                )

        steps = (count + UNROLL // 2 - 1) // UNROLL

        @pl.loop(0, steps)
        def _(step, groups=groups):
            groups(step * UNROLL, UNROLL)

        @pl.when(count > steps * UNROLL)
        def _(steps=steps, groups=groups):
            groups(steps * UNROLL, UNROLL // 2)

    if closes:
        for target in range(total_ref.shape[0]):
            row, col = divmod(target, CCOLS)
            out_ref[row * edge : (row + 1) * edge, col * edge : (col + 1) * edge] = total_ref[
                target
            ].astype(out_ref.dtype)


def per_device(a_blocks, a_rows, b_blocks, b_cols, pair_list, pair_count, row_order):
    n_row, n_col = lax.axis_size("row"), lax.axis_size("col")
    n_stops, n_pairs = pair_list.shape[2], pair_list.shape[4]
    sizes = Sizes(
        n_stops,
        n_pairs,
        a_blocks.shape[2],
        b_blocks.shape[2],
        row_order.shape[1],
        n_col,
        a_blocks.shape[3],
    )
    row = lax.axis_index("row")
    edge, sums = sizes.edge, (sizes.n_rows * CCOLS, sizes.edge, sizes.edge)
    reach = n_col + n_stops - 2
    chips = (reach + 1) // 2
    evens, odds = range(2, chips + 1, 2), range(1, chips + 1, 2)
    parts = range(PARTS)

    def from_ahead(block, axis, distance):
        size = lax.axis_size(axis)
        return lax.ppermute(block, axis, [((i + distance) % size, i) for i in range(size)])

    def swap(bit, lower, upper, skip=0):
        mine = lower if lower is upper else jnp.where(row // bit % 2 == 1, upper, lower)
        mine = mine[skip:]
        return lax.ppermute(mine, "row", [(i ^ bit, i) for i in range(n_row)])

    def both(distance):
        return (distance, distance)

    def swapped(j):
        ahead = 2 * j + 1, 2 * j - 1
        return tuple(d if 1 <= d <= reach else None for d in ahead)

    own = pack(sizes, b_blocks, b_cols)
    even = {j: [from_ahead(part, "row", 2 * j) for part in own] for j in range(2, chips + 2, 2)}
    left_ids, left_own = a_rows.reshape(1, -1), a_blocks.reshape(-1, edge)
    left_ids = [left_ids] + [from_ahead(left_ids, "col", j) for j in range(1, n_col)]
    lefts = [left_own] + [from_ahead(left_own, "col", j) for j in range(1, n_col)]
    words = kernel_call(
        functools.partial(prepare_kernel, sizes),
        jax.ShapeDtypeStruct((PARTS * n_stops, sizes.width), jnp.int32),
        [pair_count.reshape(1, -1), row_order, pair_list.reshape(2 * n_stops, n_pairs).T]
        + left_ids,
        flops=1 << 34,
    )

    def wait(part, *others):
        arrived, others = lax.optimization_barrier(([even[j][part] for j in even], others))
        for j, block in zip(even, arrived):
            even[j][part] = block
        return others

    def pass_on(part):
        sets = {0: own, **even}
        return {j: swap(2, sets[j + 1][part], sets[j - 1][part]) for j in odds}

    def add(total, pieces, closes=False):
        rights = list({id(piece[0]): piece[0] for piece in pieces}.values())
        places = {id(block): place for place, block in enumerate(rights)}
        layout = tuple((places[id(piece[0])], *piece[1:]) for piece in pieces)
        if closes:
            out_shape = jax.ShapeDtypeStruct((sizes.n_rows * edge, CCOLS * edge), jnp.bfloat16)
        else:
            out_shape = jax.ShapeDtypeStruct(sums, jnp.float32)
        if total is None:
            left_shape = ((sizes.zero_slot + 1) * edge, edge)
            out_shape = [out_shape, jax.ShapeDtypeStruct(left_shape, b_blocks.dtype)]
        lines = round_up(len(rights), 8)
        return kernel_call(
            functools.partial(
                products_kernel, sizes, len(rights), layout, total is None, closes
            ),
            out_shape,
            (lefts if total is None else [left_all])
            + rights
            + ([] if total is None else [total]),
            [words],
            [
                pltpu.VMEM((lines, 128), jnp.int32),
                pltpu.SMEM((lines, 128), jnp.int32),
                pltpu.SemaphoreType.DMA,
            ]
            + ([pltpu.VMEM(sums, jnp.float32)] if closes else []),
        )

    def pieces_of(j, part, block):
        skip = HEAD_STEP if j in evens else 0
        theirs = swap(1, block, block, skip)
        return [
            (block, HEAD, part, both(2 * j)),
            (theirs, HEAD - skip, part, swapped(j)),
        ]

    odd = {}
    (words,) = wait(0, words)
    odd[0] = pass_on(0)
    own_first, own_last = pieces_of(0, 0, own[0]), pieces_of(0, 1, own[1])
    pieces = own_first + own_last[:1]
    pieces += [piece for j in evens for piece in pieces_of(j, 0, even[j][0])]
    total, left_all = add(None, pieces)
    odd[0], total = wait(1, odd[0], total)
    odd[1] = pass_on(1)
    pieces = own_last[1:]
    pieces += [piece for j in odds for piece in pieces_of(j, 0, odd[0][j])]
    pieces += [piece for j in evens for piece in pieces_of(j, 1, even[j][1])]
    total = add(total, pieces)
    odd[1], total = lax.optimization_barrier((odd[1], total))
    pieces = [piece for j in odds for piece in pieces_of(j, 1, odd[1][j])]
    return add(total, pieces, closes=True)


def solution(mesh):
    placed = (
        P("row", "col", None, None, None),
        P("row", "col", None),
        P("row", "col", None, None, None),
        P("row", "col", None),
        P("row", "col", None, None, None),
        P("row", "col", None),
        P("row", None),
    )
    return jax.shard_map(
        per_device, mesh=mesh, in_specs=placed, out_specs=P("row", "col"), check_vma=False
    )
```

profile of v0, /device:TPU:31, one launch (start us, length us, event | category | flops | bytes accessed | tf_op | source)
XLA Modules:
  0.0 52.5 jit_solution(9866792121740591401)
XLA Ops:
  0.0 0.0 copy-start
  0.0 1.2 %copy-done = bf16[1,1,32,128,128]{4,3,2,1,0:T(8,128)(2,1)S(1)} copy-done((bf16[1,1,32,128,128]{4,3,2,1,0:T(8,128)(2,1)S(1)}, bf16[1,1,32,128,128]{4,3,2,1,0:T(8,128)(2,1)}, u32[]{:S(2)}) %copy-start) | copy-done | bytes 1048600
  1.2 0.0 copy-start.2
  1.2 0.7 %copy-done.2 = s32[1,1,32]{2,1,0:T(1,128)S(1)} copy-done((s32[1,1,32]{2,1,0:T(1,128)S(1)}, s32[1,1,32]{2,1,0:T(1,128)}, u32[]{:S(2)}) %copy-start.2) | copy-done | bytes 152
  1.9 0.4 shard_map.73
  2.3 0.7 %collective-permute-start.3 = (bf16[1952,128]{1,0:T(8,128)(2,1)S(1)}, bf16[1952,128]{1,0:T(8,128)(2,1)S(1)}, u32[]{:S(2)}, u32[]{:S(2)}) collective-permute-start(bf16[1952,128]{1,0:T(8,128)(2,1)S(1)} %get-tuple-element.16.refs_2_), channel_id=1, source_target_pairs={{2,0},{0,2},{6,4},{4,6},{10,8},{8,10},{14,12},{12,14},{18,16},{16,... | collective-permute-start | bytes 1499144 | tf_op jit(solution)/shard_map/ppermute | solution.py:258
  3.0 0.2 collective-permute-start
  3.2 0.2 collective-permute-start.1
  3.4 1.2 %collective-permute-start.2 = (bf16[2048,128]{1,0:T(8,128)(2,1)}, bf16[2048,128]{1,0:T(8,128)(2,1)S(1)}, u32[]{:S(2)}, u32[]{:S(2)}) collective-permute-start(bf16[2048,128]{1,0:T(8,128)(2,1)} %bitcast.7), channel_id=1, source_target_pairs={{1,0},{0,1},{3,2},{2,3},{5,4},{4,5},{7,6},{6,7},{9,8},{8,9},{11,10... | collective-permute-start | bytes 1572872 | tf_op jit(solution)/shard_map/ppermute | solution.py:253
  4.7 0.2 collective-permute-start.5
  4.9 0.7 %reshape.21 = s32[8,256]{1,0:T(8,128)S(1)} reshape(s32[1,1,4,2,256]{4,3,2,1,0:T(2,128)} %param.11) | data formatting | bytes 16384 | tf_op jit(solution)/shard_map/reshape | solution.py:275
  5.6 0.1 copy.9
  5.7 0.1 collective-permute-done.1.refs_1_
  5.7 0.0 copy-start.3
  5.7 0.7 %copy-done.3 = s32[1,1,4]{2,1,0:T(1,128)S(1)} copy-done((s32[1,1,4]{2,1,0:T(1,128)S(1)}, s32[1,1,4]{2,1,0:T(1,128)}, u32[]{:S(2)}) %copy-start.3) | copy-done | bytes 40
  6.4 0.0 copy-start.4
  6.4 0.7 %copy-done.4 = s32[1,4]{1,0:T(1,128)S(1)} copy-done((s32[1,4]{1,0:T(1,128)S(1)}, s32[1,4]{1,0:T(1,128)}, u32[]{:S(2)}) %copy-start.4) | copy-done | bytes 40
  7.1 0.0 copy-start.5
  7.1 0.7 %copy-done.5 = s32[1,1,16]{2,1,0:T(1,128)S(1)} copy-done((s32[1,1,16]{2,1,0:T(1,128)S(1)}, s32[1,1,16]{2,1,0:T(1,128)}, u32[]{:S(2)}) %copy-start.5) | copy-done | bytes 88
  7.7 2.9 %shard_map.74.words_ref = s32[8,256]{1,0:T(8,128)S(1)} custom-call(s32[1,4]{1,0:T(1,128)S(1)} %bitcast.11, s32[1,4]{1,0:T(1,128)S(1)} %copy-done.4, s32[256,8]{1,0:T(8,128)S(1)} %bitcast.9, s32[1,16]{1,0:T(1,128)S(1)} %bitcast.13, s32[1,16]{1,0:T(1,128)S(1)} %collective-permute-done.1.refs_1_), custom_call_target="tpu_custom_call" | custom-call | flops 17179869184 | bytes 128 | tf_op jit(solution)/shard_map/pallas_call | solution.py:49
  10.6 0.0 copy-start.1
  10.6 7.2 %collective-permute-done.refs_5_ = bf16[1952,128]{1,0:T(8,128)(2,1)S(1)} collective-permute-done((bf16[1952,128]{1,0:T(8,128)(2,1)S(1)}, bf16[1952,128]{1,0:T(8,128)(2,1)S(1)}, u32[]{:S(2)}, u32[]{:S(2)}) %collective-permute-start) | collective-permute-done | bytes 499744 | tf_op jit(solution)/shard_map/ppermute | solution.py:253
  17.8 0.1 broadcast_select_fusion.1
  17.9 0.3 collective-permute-start.6
  18.2 1.6 %collective-permute-start.4 = (bf16[1936,128]{1,0:T(8,128)(2,1)S(1)}, bf16[1936,128]{1,0:T(8,128)(2,1)S(1)}, u32[]{:S(2)}, u32[]{:S(2)}) collective-permute-start(bf16[1936,128]{1,0:T(8,128)(2,1)S(1)} %slice.6), channel_id=1, source_target_pairs={{2,0},{0,2},{6,4},{4,6},{10,8},{8,10},{14,12},{12,14},{18,16},{16,... | collective-permute-start | bytes 1486856 | tf_op jit(solution)/shard_map/ppermute | solution.py:258
  19.9 0.0 collective-permute-done.3.refs_3_
  19.9 0.1 collective-permute-start.8
  20.0 0.0 collective-permute-done.2.refs_1_
  20.0 1.4 %collective-permute-done.4.refs_6_ = bf16[1936,128]{1,0:T(8,128)(2,1)S(1)} collective-permute-done((bf16[1936,128]{1,0:T(8,128)(2,1)S(1)}, bf16[1936,128]{1,0:T(8,128)(2,1)S(1)}, u32[]{:S(2)}, u32[]{:S(2)}) %collective-permute-start.4) | collective-permute-done | bytes 495648 | tf_op jit(solution)/shard_map/ppermute | solution.py:258
  21.4 0.0 copy-done.1
  21.4 4.2 %shard_map.75 = (f32[32,128,128]{2,1,0:T(8,128)S(1)}, bf16[4224,128]{1,0:T(8,128)(2,1)S(1)}) custom-call(s32[8,256]{1,0:T(8,128)S(1)} %shard_map.74.words_ref, bf16[2048,128]{1,0:T(8,128)(2,1)S(1)} %bitcast.8, bf16[2048,128]{1,0:T(8,128)(2,1)S(1)} %collective-permute-done.2.refs_1_, bf16[1952,128]{1,0:T(8,128)(2,1)S(1)} %get-tuple-element.16.refs_2_, ...), custom_call_target="tpu_custom_call" | custom-call | flops 128 | bytes 128 | tf_op jit(solution)/shard_map/pallas_call | solution.py:49
  25.6 4.3 %collective-permute-done.5.refs_4_ = bf16[2208,128]{1,0:T(8,128)(2,1)S(1)} collective-permute-done((bf16[2208,128]{1,0:T(8,128)(2,1)S(1)}, bf16[2208,128]{1,0:T(8,128)(2,1)S(1)}, u32[]{:S(2)}, u32[]{:S(2)}) %collective-permute-start.5) | collective-permute-done | bytes 565280 | tf_op jit(solution)/shard_map/ppermute | solution.py:253
  29.9 0.0 collective-permute-done.6.refs_2_
  29.9 0.1 broadcast_select_fusion
  30.0 0.3 collective-permute-start.7
  30.3 2.2 %collective-permute-start.10 = (bf16[2192,128]{1,0:T(8,128)(2,1)S(1)}, bf16[2192,128]{1,0:T(8,128)(2,1)S(1)}, u32[]{:S(2)}, u32[]{:S(2)}) collective-permute-start(bf16[2192,128]{1,0:T(8,128)(2,1)S(1)} %slice.7), channel_id=1, source_target_pairs={{2,0},{0,2},{6,4},{4,6},{10,8},{8,10},{14,12},{12,14},{18,16},{16,... | collective-permute-start | bytes 1683464 | tf_op jit(solution)/shard_map/ppermute | solution.py:258
  32.5 0.1 collective-permute-start.9
  32.6 0.0 collective-permute-done.8.refs_1_
  32.6 2.2 %collective-permute-done.9.refs_3_ = bf16[1952,128]{1,0:T(8,128)(2,1)S(1)} collective-permute-done((bf16[1952,128]{1,0:T(8,128)(2,1)S(1)}, bf16[1952,128]{1,0:T(8,128)(2,1)S(1)}, u32[]{:S(2)}, u32[]{:S(2)}) %collective-permute-start.9) | collective-permute-done | bytes 499744 | tf_op jit(solution)/shard_map/ppermute | solution.py:258
  34.8 0.0 collective-permute-done.10.refs_5_
  34.8 6.6 %shard_map.76.refs_3_ = f32[32,128,128]{2,1,0:T(8,128)S(1)} custom-call(s32[8,256]{1,0:T(8,128)S(1)} %shard_map.74.words_ref, bf16[4224,128]{1,0:T(8,128)(2,1)S(1)} %get-tuple-element.20.refs_0_, bf16[2208,128]{1,0:T(8,128)(2,1)S(1)} %collective-permute-done.8.refs_1_, bf16[1952,128]{1,0:T(8,128)(2,1)S(1)} %collective-permute-done.6.refs_2_, ...), custom_call_target="tpu_custom_call" | custom-call | flops 128 | bytes 128 | tf_op jit(solution)/shard_map/pallas_call | solution.py:49
  41.4 1.1 %collective-permute-done.7.refs_1_ = bf16[2208,128]{1,0:T(8,128)(2,1)S(1)} collective-permute-done((bf16[2208,128]{1,0:T(8,128)(2,1)S(1)}, bf16[2208,128]{1,0:T(8,128)(2,1)S(1)}, u32[]{:S(2)}, u32[]{:S(2)}) %collective-permute-start.7) | collective-permute-done | bytes 565280 | tf_op jit(solution)/shard_map/ppermute | solution.py:258
  42.5 2.7 %collective-permute-start.11 = (bf16[2208,128]{1,0:T(8,128)(2,1)S(1)}, bf16[2208,128]{1,0:T(8,128)(2,1)S(1)}, u32[]{:S(2)}, u32[]{:S(2)}) collective-permute-start(bf16[2208,128]{1,0:T(8,128)(2,1)S(1)} %collective-permute-done.7.refs_1_), channel_id=1, source_target_pairs={{2,0},{0,2},{6,4},{4,6},{10,8},{8,10},{14,12},{12,14},{18,16},{16,... | collective-permute-start | bytes 1695752 | tf_op jit(solution)/shard_map/ppermute | solution.py:258
  45.3 1.6 %collective-permute-done.11.refs_2_ = bf16[2208,128]{1,0:T(8,128)(2,1)S(1)} collective-permute-done((bf16[2208,128]{1,0:T(8,128)(2,1)S(1)}, bf16[2208,128]{1,0:T(8,128)(2,1)S(1)}, u32[]{:S(2)}, u32[]{:S(2)}) %collective-permute-start.11) | collective-permute-done | bytes 565280 | tf_op jit(solution)/shard_map/ppermute | solution.py:258
  46.9 5.5 %shard_map.77 = bf16[512,1024]{1,0:T(8,128)(2,1)} custom-call(s32[8,256]{1,0:T(8,128)S(1)} %shard_map.74.words_ref, bf16[4224,128]{1,0:T(8,128)(2,1)S(1)} %get-tuple-element.20.refs_0_, bf16[2208,128]{1,0:T(8,128)(2,1)S(1)} %collective-permute-done.7.refs_1_, bf16[2208,128]{1,0:T(8,128)(2,1)S(1)} %collective-permute-done.11.refs_2_, ...), custom_call_target="tpu_custom_call" | custom-call | flops 128 | bytes 128 | tf_op jit(solution)/shard_map/pallas_call | solution.py:49
  (2 shorter events, 0.1 us)
Async XLA Ops:
  0.0 1.2 %copy-start = (bf16[1,1,32,128,128]{4,3,2,1,0:T(8,128)(2,1)S(1)}, bf16[1,1,32,128,128]{4,3,2,1,0:T(8,128)(2,1)}, u32[]{:S(2)}) copy-start(bf16[1,1,32,128,128]{4,3,2,1,0:T(8,128)(2,1)} %param.9) | copy-start | bytes 3145732
  1.2 0.7 %copy-start.2 = (s32[1,1,32]{2,1,0:T(1,128)S(1)}, s32[1,1,32]{2,1,0:T(1,128)}, u32[]{:S(2)}) copy-start(s32[1,1,32]{2,1,0:T(1,128)} %param.10) | copy-start | bytes 388
  2.3 17.6 %collective-permute-start.3 = (bf16[1952,128]{1,0:T(8,128)(2,1)S(1)}, bf16[1952,128]{1,0:T(8,128)(2,1)S(1)}, u32[]{:S(2)}, u32[]{:S(2)}) collective-permute-start(bf16[1952,128]{1,0:T(8,128)(2,1)S(1)} %get-tuple-element.16.refs_2_), channel_id=1, source_target_pairs={{2,0},{0,2},{6,4},{4,6},{10,8},{8,10},{14,12},{12,14},{18,16},{16,... | collective-permute-start | bytes 1499144 | tf_op jit(solution)/shard_map/ppermute | solution.py:258
  3.0 14.8 %collective-permute-start = (bf16[1952,128]{1,0:T(8,128)(2,1)S(1)}, bf16[1952,128]{1,0:T(8,128)(2,1)S(1)}, u32[]{:S(2)}, u32[]{:S(2)}) collective-permute-start(bf16[1952,128]{1,0:T(8,128)(2,1)S(1)} %get-tuple-element.16.refs_2_), channel_id=1, source_target_pairs={{8,0},{10,2},{12,4},{14,6},{16,8},{18,10},{20,12},{22,14},{24,16},... | collective-permute-start | bytes 1499144 | tf_op jit(solution)/shard_map/ppermute | solution.py:253
  3.2 2.5 %collective-permute-start.1 = (s32[1,16]{1,0:T(1,128)}, s32[1,16]{1,0:T(1,128)S(1)}, u32[]{:S(2)}, u32[]{:S(2)}) collective-permute-start(s32[1,16]{1,0:T(1,128)} %bitcast.12), channel_id=1, source_target_pairs={{1,0},{0,1},{3,2},{2,3},{5,4},{4,5},{7,6},{6,7},{9,8},{8,9},{11,10... | collective-permute-start | bytes 200 | tf_op jit(solution)/shard_map/ppermute | solution.py:253
  3.4 16.5 %collective-permute-start.2 = (bf16[2048,128]{1,0:T(8,128)(2,1)}, bf16[2048,128]{1,0:T(8,128)(2,1)S(1)}, u32[]{:S(2)}, u32[]{:S(2)}) collective-permute-start(bf16[2048,128]{1,0:T(8,128)(2,1)} %bitcast.7), channel_id=1, source_target_pairs={{1,0},{0,1},{3,2},{2,3},{5,4},{4,5},{7,6},{6,7},{9,8},{8,9},{11,10... | collective-permute-start | bytes 1572872 | tf_op jit(solution)/shard_map/ppermute | solution.py:253
  4.7 25.2 %collective-permute-start.5 = (bf16[2208,128]{1,0:T(8,128)(2,1)S(1)}, bf16[2208,128]{1,0:T(8,128)(2,1)S(1)}, u32[]{:S(2)}, u32[]{:S(2)}) collective-permute-start(bf16[2208,128]{1,0:T(8,128)(2,1)S(1)} %get-tuple-element.18.refs_4_), channel_id=1, source_target_pairs={{8,0},{10,2},{12,4},{14,6},{16,8},{18,10},{20,12},{22,14},{24,16},... | collective-permute-start | bytes 1695752 | tf_op jit(solution)/shard_map/ppermute | solution.py:253
  5.7 0.7 %copy-start.3 = (s32[1,1,4]{2,1,0:T(1,128)S(1)}, s32[1,1,4]{2,1,0:T(1,128)}, u32[]{:S(2)}) copy-start(s32[1,1,4]{2,1,0:T(1,128)} %param.12) | copy-start | bytes 52
  6.4 0.7 %copy-start.4 = (s32[1,4]{1,0:T(1,128)S(1)}, s32[1,4]{1,0:T(1,128)}, u32[]{:S(2)}) copy-start(s32[1,4]{1,0:T(1,128)} %order_ref.1) | copy-start | bytes 52
  7.1 0.7 %copy-start.5 = (s32[1,1,16]{2,1,0:T(1,128)S(1)}, s32[1,1,16]{2,1,0:T(1,128)}, u32[]{:S(2)}) copy-start(s32[1,1,16]{2,1,0:T(1,128)} %param.8) | copy-start | bytes 196
  10.6 10.8 %copy-start.1 = (bf16[1,1,16,128,128]{4,3,2,1,0:T(8,128)(2,1)S(1)}, bf16[1,1,16,128,128]{4,3,2,1,0:T(8,128)(2,1)}, u32[]{:S(2)}) copy-start(bf16[1,1,16,128,128]{4,3,2,1,0:T(8,128)(2,1)} %param.7) | copy-start | bytes 1572868
  17.9 12.1 %collective-permute-start.6 = (bf16[1952,128]{1,0:T(8,128)(2,1)S(1)}, bf16[1952,128]{1,0:T(8,128)(2,1)S(1)}, u32[]{:S(2)}, u32[]{:S(2)}) collective-permute-start(bf16[1952,128]{1,0:T(8,128)(2,1)S(1)} %broadcast_select_fusion.1), channel_id=1, source_target_pairs={{4,0},{6,2},{0,4},{2,6},{12,8},{14,10},{8,12},{10,14},{20,16},{22,... | collective-permute-start | bytes 1499144 | tf_op jit(solution)/shard_map/ppermute | solution.py:258
  18.2 3.1 %collective-permute-start.4 = (bf16[1936,128]{1,0:T(8,128)(2,1)S(1)}, bf16[1936,128]{1,0:T(8,128)(2,1)S(1)}, u32[]{:S(2)}, u32[]{:S(2)}) collective-permute-start(bf16[1936,128]{1,0:T(8,128)(2,1)S(1)} %slice.6), channel_id=1, source_target_pairs={{2,0},{0,2},{6,4},{4,6},{10,8},{8,10},{14,12},{12,14},{18,16},{16,... | collective-permute-start | bytes 1486856 | tf_op jit(solution)/shard_map/ppermute | solution.py:258
  19.9 12.7 %collective-permute-start.8 = (bf16[2208,128]{1,0:T(8,128)(2,1)S(1)}, bf16[2208,128]{1,0:T(8,128)(2,1)S(1)}, u32[]{:S(2)}, u32[]{:S(2)}) collective-permute-start(bf16[2208,128]{1,0:T(8,128)(2,1)S(1)} %get-tuple-element.18.refs_4_), channel_id=1, source_target_pairs={{2,0},{0,2},{6,4},{4,6},{10,8},{8,10},{14,12},{12,14},{18,16},{16,... | collective-permute-start | bytes 1695752 | tf_op jit(solution)/shard_map/ppermute | solution.py:258
  30.0 12.5 %collective-permute-start.7 = (bf16[2208,128]{1,0:T(8,128)(2,1)S(1)}, bf16[2208,128]{1,0:T(8,128)(2,1)S(1)}, u32[]{:S(2)}, u32[]{:S(2)}) collective-permute-start(bf16[2208,128]{1,0:T(8,128)(2,1)S(1)} %broadcast_select_fusion), channel_id=1, source_target_pairs={{4,0},{6,2},{0,4},{2,6},{12,8},{14,10},{8,12},{10,14},{20,16},{22,... | collective-permute-start | bytes 1695752 | tf_op jit(solution)/shard_map/ppermute | solution.py:258
  30.3 4.5 %collective-permute-start.10 = (bf16[2192,128]{1,0:T(8,128)(2,1)S(1)}, bf16[2192,128]{1,0:T(8,128)(2,1)S(1)}, u32[]{:S(2)}, u32[]{:S(2)}) collective-permute-start(bf16[2192,128]{1,0:T(8,128)(2,1)S(1)} %slice.7), channel_id=1, source_target_pairs={{2,0},{0,2},{6,4},{4,6},{10,8},{8,10},{14,12},{12,14},{18,16},{16,... | collective-permute-start | bytes 1683464 | tf_op jit(solution)/shard_map/ppermute | solution.py:258
  32.5 2.3 %collective-permute-start.9 = (bf16[1952,128]{1,0:T(8,128)(2,1)S(1)}, bf16[1952,128]{1,0:T(8,128)(2,1)S(1)}, u32[]{:S(2)}, u32[]{:S(2)}) collective-permute-start(bf16[1952,128]{1,0:T(8,128)(2,1)S(1)} %collective-permute-done.6.refs_2_), channel_id=1, source_target_pairs={{2,0},{0,2},{6,4},{4,6},{10,8},{8,10},{14,12},{12,14},{18,16},{16,... | collective-permute-start | bytes 1499144 | tf_op jit(solution)/shard_map/ppermute | solution.py:258
  42.5 4.3 %collective-permute-start.11 = (bf16[2208,128]{1,0:T(8,128)(2,1)S(1)}, bf16[2208,128]{1,0:T(8,128)(2,1)S(1)}, u32[]{:S(2)}, u32[]{:S(2)}) collective-permute-start(bf16[2208,128]{1,0:T(8,128)(2,1)S(1)} %collective-permute-done.7.refs_1_), channel_id=1, source_target_pairs={{2,0},{0,2},{6,4},{4,6},{10,8},{8,10},{14,12},{12,14},{18,16},{16,... | collective-permute-start | bytes 1695752 | tf_op jit(solution)/shard_map/ppermute | solution.py:258
where the time goes:
time: 53.4 us; the launch traced here: 52.5 us
  Pallas kernels  19.6 us (37%)
  waiting for transfers between devices  17.9 us (34%)
  starting transfers between devices  9.9 us (19%)
  local copies, waits for them, and re-layouts  4.75 us (9%)
    pallas_call x5, Pallas kernels, kernel_call(): pl.pallas_call(kernel, out_shape=out_shape, grid_spec=pltpu.PrefetchScala...  19.6 us
    ppermute x4, waiting for transfers between devices, from_ahead(): lax.ppermute(block, axis, [((i + distance) % size, i) for i in range(size)])  11.6 us
    ppermute x8, starting transfers between devices, swap(): return lax.ppermute(mine, 'row', [(i ^ bit, i) for i in range(n_row)])  8.1 us
    ppermute x8, waiting for transfers between devices, swap(): return lax.ppermute(mine, 'row', [(i ^ bit, i) for i in range(n_row)])  6.32 us
    unnamed x12, local copies, waits for them, and re-layouts  3.85 us
    ppermute x4, starting transfers between devices, from_ahead(): lax.ppermute(block, axis, [((i + distance) % size, i) for i in range(size)])  1.8 us
  transfers between devices with their start and end apart: 12, of which 7 were waited for; matrix products, arithmetic and copies ran while one was open for 2% of the time, Pallas kernels for 26%

commit v1 on v0

--- a/solution.py
+++ b/solution.py
@@ -331,7 +331,7 @@
     pieces = own_first + own_last[:1]
     pieces += [piece for j in evens for piece in pieces_of(j, 0, even[j][0])]
     total, left_all = add(None, pieces)
-    odd[0], total = wait(1, odd[0], total)
+    (total,) = wait(1, total)
     odd[1] = pass_on(1)
     pieces = own_last[1:]
     pieces += [piece for j in odds for piece in pieces_of(j, 0, odd[0][j])]

time: 53.4 us -> 53.6 us (level)
  the two profiles are of different devices: /device:TPU:31 before, /device:TPU:24 now
where the time goes in v1:
time: 53.6 us; the launch traced here: 53.1 us
  Pallas kernels  20.2 us (38%)
  waiting for transfers between devices  19.5 us (36%)
  starting transfers between devices  7.38 us (14%)
  local copies, waits for them, and re-layouts  5.53 us (10%)
    pallas_call x5, Pallas kernels, kernel_call(): pl.pallas_call(kernel, out_shape=out_shape, grid_spec=pltpu.PrefetchScala...  20.2 us
    ppermute x8, waiting for transfers between devices, swap(): return lax.ppermute(mine, 'row', [(i ^ bit, i) for i in range(n_row)])  9.86 us
    ppermute x4, waiting for transfers between devices, from_ahead(): lax.ppermute(block, axis, [((i + distance) % size, i) for i in range(size)])  9.68 us
    ppermute x8, starting transfers between devices, swap(): return lax.ppermute(mine, 'row', [(i ^ bit, i) for i in range(n_row)])  4.4 us
    unnamed x12, local copies, waits for them, and re-layouts  3.85 us
    ppermute x4, starting transfers between devices, from_ahead(): lax.ppermute(block, axis, [((i + distance) % size, i) for i in range(size)])  2.98 us
  transfers between devices with their start and end apart: 12, of which 8 were waited for; matrix products, arithmetic and copies ran while one was open for 3% of the time, Pallas kernels for 27%

profile of v1, /device:TPU:24, one launch (start us, length us, event | category | flops | bytes accessed | tf_op | source)
XLA Modules:
  0.0 53.1 jit_solution(16659186302117528231)
XLA Ops:
  0.0 0.0 copy-start
  0.0 1.2 %copy-done = bf16[1,1,32,128,128]{4,3,2,1,0:T(8,128)(2,1)S(1)} copy-done((bf16[1,1,32,128,128]{4,3,2,1,0:T(8,128)(2,1)S(1)}, bf16[1,1,32,128,128]{4,3,2,1,0:T(8,128)(2,1)}, u32[]{:S(2)}) %copy-start) | copy-done | bytes 1048600
  1.2 0.0 copy-start.2
  1.2 0.7 %copy-done.2 = s32[1,1,32]{2,1,0:T(1,128)S(1)} copy-done((s32[1,1,32]{2,1,0:T(1,128)S(1)}, s32[1,1,32]{2,1,0:T(1,128)}, u32[]{:S(2)}) %copy-start.2) | copy-done | bytes 152
  1.9 0.4 shard_map.73
  2.3 0.1 collective-permute-start.3
  2.4 0.5 collective-permute-start
  2.9 1.5 %collective-permute-start.1 = (s32[1,16]{1,0:T(1,128)}, s32[1,16]{1,0:T(1,128)S(1)}, u32[]{:S(2)}, u32[]{:S(2)}) collective-permute-start(s32[1,16]{1,0:T(1,128)} %bitcast.12), channel_id=1, source_target_pairs={{1,0},{0,1},{3,2},{2,3},{5,4},{4,5},{7,6},{6,7},{9,8},{8,9},{11,10... | collective-permute-start | bytes 200 | tf_op jit(solution)/shard_map/ppermute | solution.py:253
  4.4 0.5 collective-permute-start.2
  4.9 0.4 collective-permute-start.5
  5.4 0.7 %reshape.21 = s32[8,256]{1,0:T(8,128)S(1)} reshape(s32[1,1,4,2,256]{4,3,2,1,0:T(2,128)} %param.11) | data formatting | bytes 16384 | tf_op jit(solution)/shard_map/reshape | solution.py:275
  6.1 0.1 copy.9
  6.2 0.4 collective-permute-done.1.refs_1_
  6.6 0.0 copy-start.3
  6.6 0.7 %copy-done.3 = s32[1,1,4]{2,1,0:T(1,128)S(1)} copy-done((s32[1,1,4]{2,1,0:T(1,128)S(1)}, s32[1,1,4]{2,1,0:T(1,128)}, u32[]{:S(2)}) %copy-start.3) | copy-done | bytes 40
  7.2 0.0 copy-start.4
  7.2 0.7 %copy-done.4 = s32[1,4]{1,0:T(1,128)S(1)} copy-done((s32[1,4]{1,0:T(1,128)S(1)}, s32[1,4]{1,0:T(1,128)}, u32[]{:S(2)}) %copy-start.4) | copy-done | bytes 40
  7.9 0.0 copy-start.5
  7.9 0.7 %copy-done.5 = s32[1,1,16]{2,1,0:T(1,128)S(1)} copy-done((s32[1,1,16]{2,1,0:T(1,128)S(1)}, s32[1,1,16]{2,1,0:T(1,128)}, u32[]{:S(2)}) %copy-start.5) | copy-done | bytes 88
  8.5 2.9 %shard_map.74.words_ref = s32[8,256]{1,0:T(8,128)S(1)} custom-call(s32[1,4]{1,0:T(1,128)S(1)} %bitcast.11, s32[1,4]{1,0:T(1,128)S(1)} %copy-done.4, s32[256,8]{1,0:T(8,128)S(1)} %bitcast.9, s32[1,16]{1,0:T(1,128)S(1)} %bitcast.13, s32[1,16]{1,0:T(1,128)S(1)} %collective-permute-done.1.refs_1_), custom_call_target="tpu_custom_call" | custom-call | flops 17179869184 | bytes 128 | tf_op jit(solution)/shard_map/pallas_call | solution.py:49
  11.4 0.0 copy-start.1
  11.4 7.0 %collective-permute-done.refs_5_ = bf16[1952,128]{1,0:T(8,128)(2,1)S(1)} collective-permute-done((bf16[1952,128]{1,0:T(8,128)(2,1)S(1)}, bf16[1952,128]{1,0:T(8,128)(2,1)S(1)}, u32[]{:S(2)}, u32[]{:S(2)}) %collective-permute-start) | collective-permute-done | bytes 499744 | tf_op jit(solution)/shard_map/ppermute | solution.py:253
  18.4 0.8 %slice.6 = bf16[1936,128]{1,0:T(8,128)(2,1)} slice(bf16[1952,128]{1,0:T(8,128)(2,1)S(1)} %collective-permute-done.refs_5_), slice={[16:1952], [0:128]} | slice | bytes 991232 | tf_op jit(solution)/shard_map/slice | solution.py:257
  19.3 0.0 collective-permute-start.4
  19.3 0.5 collective-permute-start.7
  19.8 0.1 broadcast_select_fusion.1
  19.8 0.0 collective-permute-done.3.refs_3_
  19.8 1.6 %collective-permute-start.8 = (bf16[1952,128]{1,0:T(8,128)(2,1)S(1)}, bf16[1952,128]{1,0:T(8,128)(2,1)S(1)}, u32[]{:S(2)}, u32[]{:S(2)}) collective-permute-start(bf16[1952,128]{1,0:T(8,128)(2,1)S(1)} %broadcast_select_fusion.1), channel_id=1, source_target_pairs={{4,0},{6,2},{0,4},{2,6},{12,8},{14,10},{8,12},{10,14},{20,16},{22,... | collective-permute-start | bytes 1499144 | tf_op jit(solution)/shard_map/ppermute | solution.py:258
  21.4 0.0 collective-permute-done.2.refs_1_
  21.4 0.8 %collective-permute-done.4.refs_6_ = bf16[1936,128]{1,0:T(8,128)(2,1)} collective-permute-done((bf16[1936,128]{1,0:T(8,128)(2,1)}, bf16[1936,128]{1,0:T(8,128)(2,1)}, u32[]{:S(2)}, u32[]{:S(2)}) %collective-permute-start.4) | collective-permute-done | bytes 495648 | tf_op jit(solution)/shard_map/ppermute | solution.py:258
  22.1 0.0 copy-done.1
  22.1 5.7 %shard_map.75 = (f32[32,128,128]{2,1,0:T(8,128)S(1)}, bf16[4224,128]{1,0:T(8,128)(2,1)S(1)}) custom-call(s32[8,256]{1,0:T(8,128)S(1)} %shard_map.74.words_ref, bf16[2048,128]{1,0:T(8,128)(2,1)S(1)} %bitcast.8, bf16[2048,128]{1,0:T(8,128)(2,1)} %collective-permute-done.2.refs_1_, bf16[1952,128]{1,0:T(8,128)(2,1)S(1)} %get-tuple-element.15.refs_2_, ...), custom_call_target="tpu_custom_call" | custom-call | flops 128 | bytes 128 | tf_op jit(solution)/shard_map/pallas_call | solution.py:49
  27.8 2.3 %collective-permute-done.5.refs_4_ = bf16[2208,128]{1,0:T(8,128)(2,1)S(1)} collective-permute-done((bf16[2208,128]{1,0:T(8,128)(2,1)S(1)}, bf16[2208,128]{1,0:T(8,128)(2,1)S(1)}, u32[]{:S(2)}, u32[]{:S(2)}) %collective-permute-start.5) | collective-permute-done | bytes 565280 | tf_op jit(solution)/shard_map/ppermute | solution.py:253
  30.1 0.1 broadcast_select_fusion
  30.2 2.2 %collective-permute-start.6 = (bf16[2208,128]{1,0:T(8,128)(2,1)S(1)}, bf16[2208,128]{1,0:T(8,128)(2,1)S(1)}, u32[]{:S(2)}, u32[]{:S(2)}) collective-permute-start(bf16[2208,128]{1,0:T(8,128)(2,1)S(1)} %broadcast_select_fusion), channel_id=1, source_target_pairs={{4,0},{6,2},{0,4},{2,6},{12,8},{14,10},{8,12},{10,14},{20,16},{22,... | collective-permute-start | bytes 1695752 | tf_op jit(solution)/shard_map/ppermute | solution.py:258
  32.4 0.1 collective-permute-start.10
  32.5 1.4 %collective-permute-done.8.refs_2_ = bf16[1952,128]{1,0:T(8,128)(2,1)S(1)} collective-permute-done((bf16[1952,128]{1,0:T(8,128)(2,1)S(1)}, bf16[1952,128]{1,0:T(8,128)(2,1)S(1)}, u32[]{:S(2)}, u32[]{:S(2)}) %collective-permute-start.8) | collective-permute-done | bytes 499744 | tf_op jit(solution)/shard_map/ppermute | solution.py:258
  33.9 0.0 collective-permute-start.9
  33.9 0.0 collective-permute-done.7.refs_1_
  33.9 1.9 %collective-permute-done.9.refs_3_ = bf16[1952,128]{1,0:T(8,128)(2,1)S(1)} collective-permute-done((bf16[1952,128]{1,0:T(8,128)(2,1)S(1)}, bf16[1952,128]{1,0:T(8,128)(2,1)S(1)}, u32[]{:S(2)}, u32[]{:S(2)}) %collective-permute-start.9) | collective-permute-done | bytes 499744 | tf_op jit(solution)/shard_map/ppermute | solution.py:258
  35.7 0.0 collective-permute-done.10.refs_5_
  35.8 5.7 %shard_map.76.refs_3_ = f32[32,128,128]{2,1,0:T(8,128)S(1)} custom-call(s32[8,256]{1,0:T(8,128)S(1)} %shard_map.74.words_ref, bf16[4224,128]{1,0:T(8,128)(2,1)S(1)} %get-tuple-element.19.refs_0_, bf16[2208,128]{1,0:T(8,128)(2,1)S(1)} %collective-permute-done.7.refs_1_, bf16[1952,128]{1,0:T(8,128)(2,1)S(1)} %collective-permute-done.8.refs_2_, ...), custom_call_target="tpu_custom_call" | custom-call | flops 128 | bytes 128 | tf_op jit(solution)/shard_map/pallas_call | solution.py:49
  41.5 3.9 %collective-permute-done.6.refs_1_ = bf16[2208,128]{1,0:T(8,128)(2,1)S(1)} collective-permute-done((bf16[2208,128]{1,0:T(8,128)(2,1)S(1)}, bf16[2208,128]{1,0:T(8,128)(2,1)S(1)}, u32[]{:S(2)}, u32[]{:S(2)}) %collective-permute-start.6) | collective-permute-done | bytes 565280 | tf_op jit(solution)/shard_map/ppermute | solution.py:258
  45.3 0.0 collective-permute-start.11
  45.3 2.0 %collective-permute-done.11.refs_2_ = bf16[2208,128]{1,0:T(8,128)(2,1)S(1)} collective-permute-done((bf16[2208,128]{1,0:T(8,128)(2,1)S(1)}, bf16[2208,128]{1,0:T(8,128)(2,1)S(1)}, u32[]{:S(2)}, u32[]{:S(2)}) %collective-permute-start.11) | collective-permute-done | bytes 565280 | tf_op jit(solution)/shard_map/ppermute | solution.py:258
  47.3 5.6 %shard_map.77 = bf16[512,1024]{1,0:T(8,128)(2,1)} custom-call(s32[8,256]{1,0:T(8,128)S(1)} %shard_map.74.words_ref, bf16[4224,128]{1,0:T(8,128)(2,1)S(1)} %get-tuple-element.19.refs_0_, bf16[2208,128]{1,0:T(8,128)(2,1)S(1)} %collective-permute-done.6.refs_1_, bf16[2208,128]{1,0:T(8,128)(2,1)S(1)} %collective-permute-done.11.refs_2_, ...), custom_call_target="tpu_custom_call" | custom-call | flops 128 | bytes 128 | tf_op jit(solution)/shard_map/pallas_call | solution.py:49
  (1 shorter events, 0.0 us)
Async XLA Ops:
  0.0 1.2 %copy-start = (bf16[1,1,32,128,128]{4,3,2,1,0:T(8,128)(2,1)S(1)}, bf16[1,1,32,128,128]{4,3,2,1,0:T(8,128)(2,1)}, u32[]{:S(2)}) copy-start(bf16[1,1,32,128,128]{4,3,2,1,0:T(8,128)(2,1)} %param.9) | copy-start | bytes 3145732
  1.2 0.7 %copy-start.2 = (s32[1,1,32]{2,1,0:T(1,128)S(1)}, s32[1,1,32]{2,1,0:T(1,128)}, u32[]{:S(2)}) copy-start(s32[1,1,32]{2,1,0:T(1,128)} %param.10) | copy-start | bytes 388
  2.3 17.5 %collective-permute-start.3 = (bf16[1952,128]{1,0:T(8,128)(2,1)S(1)}, bf16[1952,128]{1,0:T(8,128)(2,1)}, u32[]{:S(2)}, u32[]{:S(2)}) collective-permute-start(bf16[1952,128]{1,0:T(8,128)(2,1)S(1)} %get-tuple-element.15.refs_2_), channel_id=1, source_target_pairs={{2,0},{0,2},{6,4},{4,6},{10,8},{8,10},{14,12},{12,14},{18,16},{16,... | collective-permute-start | bytes 1499144 | tf_op jit(solution)/shard_map/ppermute | solution.py:258
  2.4 16.1 %collective-permute-start = (bf16[1952,128]{1,0:T(8,128)(2,1)S(1)}, bf16[1952,128]{1,0:T(8,128)(2,1)S(1)}, u32[]{:S(2)}, u32[]{:S(2)}) collective-permute-start(bf16[1952,128]{1,0:T(8,128)(2,1)S(1)} %get-tuple-element.15.refs_2_), channel_id=1, source_target_pairs={{8,0},{10,2},{12,4},{14,6},{16,8},{18,10},{20,12},{22,14},{24,16},... | collective-permute-start | bytes 1499144 | tf_op jit(solution)/shard_map/ppermute | solution.py:253
  2.9 3.7 %collective-permute-start.1 = (s32[1,16]{1,0:T(1,128)}, s32[1,16]{1,0:T(1,128)S(1)}, u32[]{:S(2)}, u32[]{:S(2)}) collective-permute-start(s32[1,16]{1,0:T(1,128)} %bitcast.12), channel_id=1, source_target_pairs={{1,0},{0,1},{3,2},{2,3},{5,4},{4,5},{7,6},{6,7},{9,8},{8,9},{11,10... | collective-permute-start | bytes 200 | tf_op jit(solution)/shard_map/ppermute | solution.py:253
  4.4 17.0 %collective-permute-start.2 = (bf16[2048,128]{1,0:T(8,128)(2,1)}, bf16[2048,128]{1,0:T(8,128)(2,1)}, u32[]{:S(2)}, u32[]{:S(2)}) collective-permute-start(bf16[2048,128]{1,0:T(8,128)(2,1)} %bitcast.7), channel_id=1, source_target_pairs={{1,0},{0,1},{3,2},{2,3},{5,4},{4,5},{7,6},{6,7},{9,8},{8,9},{11,10... | collective-permute-start | bytes 1572872 | tf_op jit(solution)/shard_map/ppermute | solution.py:253
  4.9 25.2 %collective-permute-start.5 = (bf16[2208,128]{1,0:T(8,128)(2,1)S(1)}, bf16[2208,128]{1,0:T(8,128)(2,1)S(1)}, u32[]{:S(2)}, u32[]{:S(2)}) collective-permute-start(bf16[2208,128]{1,0:T(8,128)(2,1)S(1)} %get-tuple-element.17.refs_4_), channel_id=1, source_target_pairs={{8,0},{10,2},{12,4},{14,6},{16,8},{18,10},{20,12},{22,14},{24,16},... | collective-permute-start | bytes 1695752 | tf_op jit(solution)/shard_map/ppermute | solution.py:253
  6.6 0.7 %copy-start.3 = (s32[1,1,4]{2,1,0:T(1,128)S(1)}, s32[1,1,4]{2,1,0:T(1,128)}, u32[]{:S(2)}) copy-start(s32[1,1,4]{2,1,0:T(1,128)} %param.12) | copy-start | bytes 52
  7.2 0.7 %copy-start.4 = (s32[1,4]{1,0:T(1,128)S(1)}, s32[1,4]{1,0:T(1,128)}, u32[]{:S(2)}) copy-start(s32[1,4]{1,0:T(1,128)} %order_ref.1) | copy-start | bytes 52
  7.9 0.7 %copy-start.5 = (s32[1,1,16]{2,1,0:T(1,128)S(1)}, s32[1,1,16]{2,1,0:T(1,128)}, u32[]{:S(2)}) copy-start(s32[1,1,16]{2,1,0:T(1,128)} %param.8) | copy-start | bytes 196
  11.4 10.7 %copy-start.1 = (bf16[1,1,16,128,128]{4,3,2,1,0:T(8,128)(2,1)S(1)}, bf16[1,1,16,128,128]{4,3,2,1,0:T(8,128)(2,1)}, u32[]{:S(2)}) copy-start(bf16[1,1,16,128,128]{4,3,2,1,0:T(8,128)(2,1)} %param.7) | copy-start | bytes 1572868
  19.3 2.9 %collective-permute-start.4 = (bf16[1936,128]{1,0:T(8,128)(2,1)}, bf16[1936,128]{1,0:T(8,128)(2,1)}, u32[]{:S(2)}, u32[]{:S(2)}) collective-permute-start(bf16[1936,128]{1,0:T(8,128)(2,1)} %slice.6), channel_id=1, source_target_pairs={{2,0},{0,2},{6,4},{4,6},{10,8},{8,10},{14,12},{12,14},{18,16},{16,... | collective-permute-start | bytes 1486856 | tf_op jit(solution)/shard_map/ppermute | solution.py:258
  19.3 14.6 %collective-permute-start.7 = (bf16[2208,128]{1,0:T(8,128)(2,1)S(1)}, bf16[2208,128]{1,0:T(8,128)(2,1)S(1)}, u32[]{:S(2)}, u32[]{:S(2)}) collective-permute-start(bf16[2208,128]{1,0:T(8,128)(2,1)S(1)} %get-tuple-element.17.refs_4_), channel_id=1, source_target_pairs={{2,0},{0,2},{6,4},{4,6},{10,8},{8,10},{14,12},{12,14},{18,16},{16,... | collective-permute-start | bytes 1695752 | tf_op jit(solution)/shard_map/ppermute | solution.py:258
  19.8 14.0 %collective-permute-start.8 = (bf16[1952,128]{1,0:T(8,128)(2,1)S(1)}, bf16[1952,128]{1,0:T(8,128)(2,1)S(1)}, u32[]{:S(2)}, u32[]{:S(2)}) collective-permute-start(bf16[1952,128]{1,0:T(8,128)(2,1)S(1)} %broadcast_select_fusion.1), channel_id=1, source_target_pairs={{4,0},{6,2},{0,4},{2,6},{12,8},{14,10},{8,12},{10,14},{20,16},{22,... | collective-permute-start | bytes 1499144 | tf_op jit(solution)/shard_map/ppermute | solution.py:258
  30.2 15.2 %collective-permute-start.6 = (bf16[2208,128]{1,0:T(8,128)(2,1)S(1)}, bf16[2208,128]{1,0:T(8,128)(2,1)S(1)}, u32[]{:S(2)}, u32[]{:S(2)}) collective-permute-start(bf16[2208,128]{1,0:T(8,128)(2,1)S(1)} %broadcast_select_fusion), channel_id=1, source_target_pairs={{4,0},{6,2},{0,4},{2,6},{12,8},{14,10},{8,12},{10,14},{20,16},{22,... | collective-permute-start | bytes 1695752 | tf_op jit(solution)/shard_map/ppermute | solution.py:258
  32.4 3.4 %collective-permute-start.10 = (bf16[2192,128]{1,0:T(8,128)(2,1)S(1)}, bf16[2192,128]{1,0:T(8,128)(2,1)S(1)}, u32[]{:S(2)}, u32[]{:S(2)}) collective-permute-start(bf16[2192,128]{1,0:T(8,128)(2,1)S(1)} %slice.7), channel_id=1, source_target_pairs={{2,0},{0,2},{6,4},{4,6},{10,8},{8,10},{14,12},{12,14},{18,16},{16,... | collective-permute-start | bytes 1683464 | tf_op jit(solution)/shard_map/ppermute | solution.py:258
  33.9 1.9 %collective-permute-start.9 = (bf16[1952,128]{1,0:T(8,128)(2,1)S(1)}, bf16[1952,128]{1,0:T(8,128)(2,1)S(1)}, u32[]{:S(2)}, u32[]{:S(2)}) collective-permute-start(bf16[1952,128]{1,0:T(8,128)(2,1)S(1)} %collective-permute-done.8.refs_2_), channel_id=1, source_target_pairs={{2,0},{0,2},{6,4},{4,6},{10,8},{8,10},{14,12},{12,14},{18,16},{16,... | collective-permute-start | bytes 1499144 | tf_op jit(solution)/shard_map/ppermute | solution.py:258
  45.3 2.0 %collective-permute-start.11 = (bf16[2208,128]{1,0:T(8,128)(2,1)S(1)}, bf16[2208,128]{1,0:T(8,128)(2,1)S(1)}, u32[]{:S(2)}, u32[]{:S(2)}) collective-permute-start(bf16[2208,128]{1,0:T(8,128)(2,1)S(1)} %collective-permute-done.6.refs_1_), channel_id=1, source_target_pairs={{2,0},{0,2},{6,4},{4,6},{10,8},{8,10},{14,12},{12,14},{18,16},{16,... | collective-permute-start | bytes 1695752 | tf_op jit(solution)/shard_map/ppermute | solution.py:258
